TPU v7x, 32 devices: a whole 2x2x4 slice. The times are simulated.
32 devices in a mesh: groups: 2 (over y), tensor: 4 (over z), dp: 2 (over x), pipe: 2 (over core).
Axes of the slice: x: 2, y: 2, z: 4, core: 2. Of those that a mesh axis runs over, the one named last changes fastest.
Arguments:
- tokens: bfloat16 [512, 16384], P(('groups', 'dp', 'pipe'), 'tensor'), parts along dimension 0, may hold values from -6 to 6
- signs: int32 [16384], P('tensor'), may hold values from -1 to 1, as said below
- exponents: int32 [512], P(('groups', 'dp', 'pipe')), parts along dimension 0, may hold values from -12 to 0
- weights: bfloat16 [16384, 18432], P('tensor', ('dp', 'pipe')), may hold values from -0.046875 to 0.046875
Outputs:
- projected: bfloat16 [512, 18432], P(('groups', 'tensor'), ('dp', 'pipe')), parts along dimension 0
There are 2 independent parts, one for each index of `groups`. A program takes and returns all parts, laid end to end along the dimension named above; an argument that names none is the same for every part. Nothing has to cross between parts.
Inputs may be any that keep to these rules, and one draw needn't show every extreme that they name: `signs`: each entry is -1 or 1.
All inputs are finite; a program needn't handle non-finite values.
Results may differ from a plain program's by a relative error of at most 0.015.
Values may be sent and summed in bfloat16 or wider, within the bound.
A program may use at most 128 MiB of HBM per device.

v0:
```python
import math

import jax
import jax.numpy as jnp
from jax import lax
from jax.sharding import PartitionSpec as P

D = 16384


def partner_2(value, axis, bit):
    mask = 2**bit
    pairs = [(source, source ^ mask) for source in range(lax.axis_size(axis))]
    return lax.ppermute(value, axis, pairs)


def sylvester(order):
    rows = jnp.arange(order, dtype=jnp.int32)[:, None]
    cols = jnp.arange(order, dtype=jnp.int32)[None, :]
    parity = jnp.zeros((order, order), jnp.int32)
    for level in range(order.bit_length() - 1):
        parity = parity + rows // 2**level % 2 * (cols // 2**level % 2)
    return (1 - 2 * (parity % 2)).astype(jnp.float32)


def shards(tokens, signs, exponents, weights):
    rows, width = tokens.shape
    members = lax.axis_size("tensor")
    signed = tokens * signs.astype(jnp.bfloat16)[None, :]
    mixed = jnp.dot(
        signed, sylvester(width).astype(jnp.bfloat16), preferred_element_type=jnp.float32
    )
    position = lax.axis_index("tensor")
    for level in range(members.bit_length() - 1):
        partner = partner_2(mixed.astype(jnp.bfloat16), "tensor", level).astype(mixed.dtype)
        upper = position // 2**level % 2
        mixed = jnp.where(upper == 0, mixed + partner, partner - mixed)
    rotated = mixed * jnp.float32(1.0 / math.sqrt(D))
    scale = jnp.exp2(jnp.float32(0.25) * exponents.astype(jnp.float32))[:, None]
    level_value = rotated / scale
    soft = jnp.clip(level_value - jnp.sin(2.0 * math.pi * level_value) / (2.0 * math.pi), -8.0, 7.0)
    quantized = (soft * scale).astype(jnp.bfloat16)
    terms = jnp.dot(
        lax.all_gather(quantized, ("dp", "pipe"), axis=0, tiled=True),
        weights,
        preferred_element_type=jnp.float32,
    )
    summed = lax.psum_scatter(terms.astype(jnp.bfloat16), "tensor", scatter_dimension=0, tiled=True)
    return summed


def solution(mesh):
    placed = (
        P(("groups", "dp", "pipe"), "tensor"),
        P("tensor"),
        P(("groups", "dp", "pipe")),
        P("tensor", ("dp", "pipe")),
    )
    return jax.shard_map(
        shards,
        mesh=mesh,
        in_specs=placed,
        out_specs=P(("groups", "tensor"), ("dp", "pipe")),
        check_vma=False,
    )
```

profile of v0, /device:TPU:0, one launch (start us, length us, event | category | flops | bytes accessed | tf_op | source)
XLA Modules:
  0.0 238.4 jit_solution(13802195268186127423)
XLA Ops:
  6.5 0.0 all-gather.2.cloned.1.call-start
  6.6 0.7 convert_element_type.30
  7.3 1.1 fusion.12.clone.5
  8.4 0.0 copy-start
  8.4 87.4 %fusion.53 = (bf16[64,4096]{1,0:T(8,128)(2,1)S(1)}, f32[64,4096]{1,0:T(8,128)S(1)}) fusion(s32[4096]{0:T(1024)S(1)} %get-tuple-element.7, s32[4096]{0:T(1024)S(1)} %get-tuple-element.8, s32[4096]{0:T(1024)S(1)} %get-tuple-element.9, s32[4096]{0:T(1024)S(1)} %get-tuple-element.10, s32[4096]{0:T(1024)S(1)} %get-tuple-element.11, ...), kind=kOutput, calls=%fused_computation.130 | convolution fusion | flops 2785280000 | bytes 2293760 | tf_op jit(solution)/shard_map/dot_general | solution.py:30
  95.8 3.1 %collective-permute-start = (bf16[64,4096]{1,0:T(8,128)(2,1)S(1)}, bf16[64,4096]{1,0:T(8,128)(2,1)S(1)}, u32[]{:S(2)}, u32[]{:S(2)}) collective-permute-start(bf16[64,4096]{1,0:T(8,128)(2,1)S(1)} %get-tuple-element.5), channel_id=1, source_target_pairs={{0,4},{4,0},{8,12},{12,8},{1,5},{5,1},{9,13},{13,9},{2,6},{6,2},{1... | collective-permute-start | bytes 1572872 | tf_op jit(solution)/shard_map/ppermute | solution.py:14
  98.9 11.9 %collective-permute-done = bf16[64,4096]{1,0:T(8,128)(2,1)S(1)} collective-permute-done((bf16[64,4096]{1,0:T(8,128)(2,1)S(1)}, bf16[64,4096]{1,0:T(8,128)(2,1)S(1)}, u32[]{:S(2)}, u32[]{:S(2)}) %collective-permute-start) | collective-permute-done | bytes 524320 | tf_op jit(solution)/shard_map/ppermute | solution.py:14
  110.8 0.2 fusion.11
  111.0 2.8 %collective-permute-start.1 = (bf16[64,4096]{1,0:T(8,128)(2,1)S(1)}, bf16[64,4096]{1,0:T(8,128)(2,1)S(1)}, u32[]{:S(2)}, u32[]{:S(2)}) collective-permute-start(bf16[64,4096]{1,0:T(8,128)(2,1)S(1)} %fusion.11), channel_id=1, source_target_pairs={{0,8},{4,12},{8,0},{12,4},{1,9},{5,13},{9,1},{13,5},{2,10},{6,14},... | collective-permute-start | bytes 1572872 | tf_op jit(solution)/shard_map/ppermute | solution.py:14
  113.8 0.0 copy-done
  113.8 22.5 %collective-permute-done.1 = bf16[64,4096]{1,0:T(8,128)(2,1)S(1)} collective-permute-done((bf16[64,4096]{1,0:T(8,128)(2,1)S(1)}, bf16[64,4096]{1,0:T(8,128)(2,1)S(1)}, u32[]{:S(2)}, u32[]{:S(2)}) %collective-permute-start.1) | collective-permute-done | bytes 524320 | tf_op jit(solution)/shard_map/ppermute | solution.py:14
  136.3 4.9 %multiply_convert_fusion = bf16[64,4096]{1,0:T(8,128)(2,1)} fusion(bf16[64,4096]{1,0:T(8,128)(2,1)S(1)} %collective-permute-done.1, f32[64,4096]{1,0:T(8,128)S(1)} %get-tuple-element.6, bf16[64,4096]{1,0:T(8,128)(2,1)S(1)} %collective-permute-done, f32[64]{0:T(128)S(1)} %multiply_exponential_fusion, pred[]{:T(512)S(6)} %eq.38, pred[]{:T(512)S(6)} %eq.37), kind=kLoop, calls=%fused_computation.18 | loop fusion | flops 4194304 | bytes 2621698 | tf_op jit(solution)/shard_map/convert_element_type | solution.py:42
  141.1 0.0 all-gather.2.cloned.1.call-update
  141.1 0.0 reduce-scatter.2.cloned.1.call-start
  141.2 23.7 %all-gather.2.cloned.1.call-done = bf16[256,4096]{1,0:T(8,128)(2,1)} async-done(((bf16[64,4096]{1,0:T(8,128)(2,1)}), bf16[256,4096]{1,0:T(8,128)(2,1)}) %all-gather.2.cloned.1.call-update) | async-done | bytes 2097168 | tf_op jit(solution)/shard_map/all_gather | solution.py:44
  164.9 18.4 %convolution_convert_fusion = bf16[256,4608]{1,0:T(8,128)(2,1)} fusion(bf16[256,4096]{1,0:T(8,128)(2,1)} %all-gather.2.cloned.1.call-done, bf16[4096,4608]{1,0:T(8,128)(2,1)} %param.7), kind=kOutput, calls=%fused_computation.9 | convolution fusion | flops 9664856064 | bytes 42205184 | tf_op jit(solution)/shard_map/dot_general | solution.py:43
  183.3 0.0 reduce-scatter.2.cloned.1.call-update
  183.3 48.2 %reduce-scatter.2.cloned.1.call-done = bf16[64,4608]{1,0:T(8,128)(2,1)} async-done(((bf16[256,4608]{1,0:T(8,128)(2,1)}), bf16[64,4608]{1,0:T(8,128)(2,1)}) %reduce-scatter.2.cloned.1.call-update) | async-done | bytes 589840 | tf_op jit(solution)/shard_map/reduce_scatter | solution.py:48
  (7 shorter events, 0.0 us)
Async XLA Ops:
  6.5 158.3 %all-gather.2.cloned.1.call-start = ((), (), s32[]{:S(2)}) async-start(), calls=%async_computation.1 | async-start | bytes 2621440 | tf_op jit(solution)/shard_map/all_gather | solution.py:44
  8.4 105.4 %copy-start = (s32[64]{0:T(128)S(1)}, s32[64]{0:T(128)}, u32[]{:S(2)}) copy-start(s32[64]{0:T(128)} %param.6) | copy-start | bytes 772
  95.8 15.0 %collective-permute-start = (bf16[64,4096]{1,0:T(8,128)(2,1)S(1)}, bf16[64,4096]{1,0:T(8,128)(2,1)S(1)}, u32[]{:S(2)}, u32[]{:S(2)}) collective-permute-start(bf16[64,4096]{1,0:T(8,128)(2,1)S(1)} %get-tuple-element.5), channel_id=1, source_target_pairs={{0,4},{4,0},{8,12},{12,8},{1,5},{5,1},{9,13},{13,9},{2,6},{6,2},{1... | collective-permute-start | bytes 1572872 | tf_op jit(solution)/shard_map/ppermute | solution.py:14
  111.0 25.3 %collective-permute-start.1 = (bf16[64,4096]{1,0:T(8,128)(2,1)S(1)}, bf16[64,4096]{1,0:T(8,128)(2,1)S(1)}, u32[]{:S(2)}, u32[]{:S(2)}) collective-permute-start(bf16[64,4096]{1,0:T(8,128)(2,1)S(1)} %fusion.11), channel_id=1, source_target_pairs={{0,8},{4,12},{8,0},{12,4},{1,9},{5,13},{9,1},{13,5},{2,10},{6,14},... | collective-permute-start | bytes 1572872 | tf_op jit(solution)/shard_map/ppermute | solution.py:14
  141.1 90.4 %reduce-scatter.2.cloned.1.call-start = ((), (), s32[]{:S(2)}) async-start(), calls=%async_computation.2 | async-start | bytes 2949120 | tf_op jit(solution)/shard_map/reduce_scatter | solution.py:48
Sparse Core Ops, SparseCore 0:
  141.3 23.5 all-gather.1
  183.4 48.0 reduce-scatter.1
where the time goes:
time: 239 us; the launch traced here: 238 us
  matrix products  106 us (44%)
  waiting for transfers between devices  106 us (44%)
  between operations  13.5 us (6%)
  other arithmetic  6.86 us (3%)
  starting transfers between devices  5.95 us (2%)
    dot_general x1, matrix products, shards(): jnp.dot(signed, sylvester(width).astype(jnp.bfloat16), preferred_element_...  87.4 us
    reduce_scatter x1, waiting for transfers between devices, shards(): lax.psum_scatter(terms.astype(jnp.bfloat16), 'tensor', scatter_dimension=...  48.2 us
    ppermute x2, waiting for transfers between devices, partner_2(): return lax.ppermute(value, axis, pairs)  34.4 us
    all_gather x1, waiting for transfers between devices, shards(): lax.all_gather(quantized, ('dp', 'pipe'), axis=0, tiled=True)  23.7 us
    dot_general x1, matrix products, shards(): jnp.dot(lax.all_gather(quantized, ('dp', 'pipe'), axis=0, tiled=True), we...  18.4 us
    ppermute x2, starting transfers between devices, partner_2(): return lax.ppermute(value, axis, pairs)  5.91 us
    convert_element_type x1, other arithmetic, shards(): quantized = (soft * scale).astype(jnp.bfloat16)  4.85 us
  transfers between devices with their start and end apart: 4, of which 4 were waited for; matrix products, arithmetic and copies ran while one was open for 0% of the time, Pallas kernels for 0%

commit v1 on v0

--- a/solution.py
+++ b/solution.py
@@ -1,11 +1,17 @@
+import functools
 import math
 
 import jax
 import jax.numpy as jnp
 from jax import lax
+from jax.experimental import pallas as pl
+from jax.experimental.pallas import tpu as pltpu
 from jax.sharding import PartitionSpec as P
 
 D = 16384
+MESH = pl.DeviceIdType.MESH
+BASE = 256
+PARTS = 2
 
 
 def partner_2(value, axis, bit):
@@ -15,17 +21,303 @@
 
 
 def sylvester(order):
-    rows = jnp.arange(order, dtype=jnp.int32)[:, None]
-    cols = jnp.arange(order, dtype=jnp.int32)[None, :]
-    parity = jnp.zeros((order, order), jnp.int32)
-    for level in range(order.bit_length() - 1):
-        parity = parity + rows // 2**level % 2 * (cols // 2**level % 2)
-    return (1 - 2 * (parity % 2)).astype(jnp.float32)
+    rows = lax.broadcasted_iota(jnp.int32, (order, order), 0)
+    cols = lax.broadcasted_iota(jnp.int32, (order, order), 1)
+    both = rows & cols
+    shift = 1
+    while shift < order.bit_length():
+        both = both ^ (both >> shift)
+        shift *= 2
+    return (1 - 2 * (both & 1)).astype(jnp.float32)
+
+
+def butterfly(values):
+    values = list(values)
+    step = 1
+    while step < len(values):
+        for low in range(len(values)):
+            if low & step == 0:
+                a, b = values[low], values[low + step]
+                values[low], values[low + step] = a + b, a - b
+        step *= 2
+    return values
+
+
+def sin_turns(turns):
+    part = turns - jnp.round(turns)
+    part = jnp.where(part > 0.25, 0.5 - part, jnp.where(part < -0.25, -0.5 - part, part))
+    angle = part * jnp.float32(2.0 * math.pi)
+    square = angle * angle
+    total = jnp.float32(-1.0 / math.factorial(11))
+    for order, sign in ((9, 1.0), (7, -1.0), (5, 1.0), (3, -1.0)):
+        total = total * square + jnp.float32(sign / math.factorial(order))
+    return angle + angle * square * total
+
+
+def fake_quantize(rotated, scale, inverse):
+    level = rotated * inverse
+    soft = jnp.clip(level - sin_turns(level) * jnp.float32(1.0 / (2.0 * math.pi)), -8.0, 7.0)
+    return (soft * scale).astype(jnp.bfloat16)
+
+
+def kernel(
+    nz, strip, tokens, signs, exponents, weights, out,
+    held, mixed, taken, levels, acts, terms, from_left, from_right,
+    weight_sem, mix_send, mix_recv, lev_send, lev_recv, x_send, x_recv,
+    core_send, core_recv, pass_send, pass_recv, right_send, right_recv, left_send, left_recv,
+):
+    rows, width = tokens.shape
+    quarter = width // nz
+    part_rows = rows // PARTS
+    strips = weights.shape[1] // strip
+    chunk = out.shape[0]
+    z = lax.axis_index("tensor")
+    x = lax.axis_index("dp")
+    core = lax.axis_index("pipe")
+    across = {"dp": 1 - x}
+    beside = {"pipe": 1 - core}
+
+    def weight_copy(s):
+        return pltpu.make_async_copy(
+            weights.at[:, pl.ds(pl.multiple_of(s * strip, strip), strip)], held.at[s], weight_sem.at[s]
+        )
+
+    barrier = pltpu.get_barrier_semaphore()
+    for k in range(1, nz):
+        pl.semaphore_signal(barrier, inc=1, device_id={"tensor": z ^ k}, device_id_type=MESH)
+    pl.semaphore_signal(barrier, inc=1, device_id=across, device_id_type=MESH)
+    pl.semaphore_signal(barrier, inc=1, device_id=beside, device_id_type=MESH)
+
+    small = sylvester(BASE).astype(jnp.bfloat16)
+    signed = signs[...].astype(jnp.bfloat16)
+
+    def mix_copy(h, k):
+        span = pl.ds(h * part_rows, part_rows)
+        return pltpu.make_async_remote_copy(
+            src_ref=mixed.at[z ^ k, span], dst_ref=taken.at[z, span],
+            send_sem=mix_send.at[h, k], recv_sem=mix_recv.at[h, k],
+            device_id={"tensor": z ^ k}, device_id_type=MESH,
+        )
+
+    for h in range(PARTS):
+        span = slice(h * part_rows, (h + 1) * part_rows)
+        blocks = []
+        for a in range(width // BASE):
+            cols = slice(a * BASE, (a + 1) * BASE)
+            blocks.append(jnp.dot(tokens[span, cols] * signed[:, cols], small, preferred_element_type=jnp.float32))
+        for a, block in enumerate(butterfly(blocks)):
+            q, at = divmod(a * BASE, quarter)
+            mixed[q, span, at:at + BASE] = (block * jnp.float32(1.0 / math.sqrt(D))).astype(jnp.bfloat16)
+        if h == 0:
+            pl.semaphore_wait(barrier, nz + 1)
+        for k in range(nz - 1, 0, -1):
+            mix_copy(h, k).start()
+        taken[z, span] = mixed[z, span]
+
+    pl.loop(0, strips)(lambda s: weight_copy(s).start())
+
+    at_row = lax.broadcasted_iota(jnp.int32, (rows, rows), 0)
+    at_col = lax.broadcasted_iota(jnp.int32, (rows, rows), 1)
+    power = jnp.sum(
+        jnp.where(at_row == at_col, 0.25 * exponents[...].astype(jnp.float32), 0.0), axis=1, keepdims=True
+    )
+    scale = jnp.exp2(power)
+    inverse = jnp.exp2(-power)
+
+    mine = (x * 2 + core) * rows
+
+    def lev_copy(h, k):
+        return pltpu.make_async_remote_copy(
+            src_ref=levels.at[z ^ k, pl.ds(h * part_rows, part_rows)],
+            dst_ref=acts.at[z, pl.ds(pl.multiple_of(mine + h * part_rows, part_rows), part_rows)],
+            send_sem=lev_send.at[h, k], recv_sem=lev_recv.at[h, k],
+            device_id={"tensor": z ^ k}, device_id_type=MESH,
+        )
+
+    def side_copy(h, k, owner_x, target, send, recv):
+        at = (owner_x * 2 + core) * rows + h * part_rows
+        ref = acts.at[z ^ k, pl.ds(pl.multiple_of(at, part_rows), part_rows)]
+        return pltpu.make_async_remote_copy(
+            src_ref=ref, dst_ref=ref, send_sem=send.at[h, k], recv_sem=recv.at[h, k],
+            device_id=target, device_id_type=MESH,
+        )
+
+    def x_copy(h, k):
+        return side_copy(h, k, x, across, x_send, x_recv)
+
+    def core_copy(h, k):
+        return side_copy(h, k, x, beside, core_send, core_recv)
+
+    def pass_copy(h, k):
+        return side_copy(h, k, 1 - x, beside, pass_send, pass_recv)
+
+    for h in range(PARTS):
+        span = slice(h * part_rows, (h + 1) * part_rows)
+        for k in range(1, nz):
+            mix_copy(h, k).wait_recv()
+        for lane in range(0, quarter, BASE):
+            lanes = slice(lane, lane + BASE)
+            whole = butterfly([taken[q, span, lanes].astype(jnp.float32) for q in range(nz)])
+            for q in range(nz):
+                levels[q, span, lanes] = fake_quantize(whole[q], scale[span], inverse[span])
+        for k in range(nz - 1, 0, -1):
+            lev_copy(h, k).start()
+        acts[z, pl.ds(pl.multiple_of(mine + h * part_rows, part_rows), part_rows)] = levels[z, span]
+        x_copy(h, 0).start()
+        core_copy(h, 0).start()
+
+    steps = [(h, 0) for h in range(PARTS)] + [(h, k) for h in range(PARTS) for k in range(1, nz)]
+    for i in range(len(steps) + 1):
+        if PARTS <= i < len(steps):
+            lev_copy(*steps[i]).wait_recv()
+            x_copy(*steps[i]).start()
+            core_copy(*steps[i]).start()
+        if i > 0:
+            x_copy(*steps[i - 1]).wait_recv()
+            pass_copy(*steps[i - 1]).start()
+    for step in steps:
+        core_copy(*step).wait_recv()
+        pass_copy(*step).wait_recv()
+
+    def right_copy(s, d):
+        return pltpu.make_async_remote_copy(
+            src_ref=terms.at[s, d], dst_ref=from_left.at[s, d],
+            send_sem=right_send.at[s, d], recv_sem=right_recv.at[s, d],
+            device_id={"tensor": lax.rem(z + 1, nz)}, device_id_type=MESH,
+        )
+
+    def left_copy(s, d):
+        return pltpu.make_async_remote_copy(
+            src_ref=terms.at[s, d], dst_ref=from_right.at[s, d],
+            send_sem=left_send.at[s, d], recv_sem=left_recv.at[s, d],
+            device_id={"tensor": lax.rem(z + nz - 1, nz)}, device_id_type=MESH,
+        )
+
+    def add_in(s, d, arrived):
+        terms[s, d] = (terms[s, d].astype(jnp.float32) + arrived[s, d].astype(jnp.float32)).astype(jnp.bfloat16)
+
+    def when_strip(s, body):
+        pl.when(jnp.logical_and(s >= 0, s < strips))(functools.partial(body, s))
+
+    def multiply(s):
+        weight_copy(s).wait()
+        total = jnp.dot(acts[0], held[s, :quarter], preferred_element_type=jnp.float32)
+        for q in range(1, nz):
+            total += jnp.dot(
+                acts[q], held[s, q * quarter:(q + 1) * quarter], preferred_element_type=jnp.float32
+            )
+        for d in range(nz):
+            terms[s, d] = total[d * chunk:(d + 1) * chunk].astype(jnp.bfloat16)
+
+    def hop(at, s):
+        @pl.when(z == at)
+        def _():
+            for d in range(nz - 1, at, -1):
+                if at > 0:
+                    right_copy(s, d).wait_recv()
+                    add_in(s, d, from_left)
+                right_copy(s, d).start()
+
+        @pl.when(z == nz - 1 - at)
+        def _():
+            for d in range(nz - 1 - at):
+                if at > 0:
+                    left_copy(s, d).wait_recv()
+                    add_in(s, d, from_right)
+                left_copy(s, d).start()
+
+    def finish(s):
+        cols = pl.ds(pl.multiple_of(s * strip, strip), strip)
+        own = terms[s, z].astype(jnp.float32)
+
+        @pl.when(z == 0)
+        def _():
+            left_copy(s, z).wait_recv()
+            out[:, cols] = (own + from_right[s, z].astype(jnp.float32)).astype(out.dtype)
+
+        @pl.when(z == nz - 1)
+        def _():
+            right_copy(s, z).wait_recv()
+            out[:, cols] = (own + from_left[s, z].astype(jnp.float32)).astype(out.dtype)
+
+        @pl.when(jnp.logical_and(z > 0, z < nz - 1))
+        def _():
+            right_copy(s, z).wait_recv()
+            left_copy(s, z).wait_recv()
+            out[:, cols] = (
+                own + from_left[s, z].astype(jnp.float32) + from_right[s, z].astype(jnp.float32)
+            ).astype(out.dtype)
+
+    @pl.loop(0, strips + nz - 1)
+    def _(t):
+        when_strip(t, multiply)
+        for at in range(nz - 1):
+            when_strip(t - at, functools.partial(hop, at))
+        when_strip(t - (nz - 1), finish)
+
+    for h in range(PARTS):
+        for k in range(nz):
+            if k > 0:
+                mix_copy(h, k).wait_send()
+                lev_copy(h, k).wait_send()
+            x_copy(h, k).wait_send()
+            core_copy(h, k).wait_send()
+            pass_copy(h, k).wait_send()
+
+    @pl.loop(0, strips)
+    def _(s):
+        for d in range(nz):
+            pl.when(z < d)(lambda d=d: right_copy(s, d).wait_send())
+            pl.when(z > d)(lambda d=d: left_copy(s, d).wait_send())
+
+
+def fused(nz, gathered, tokens, signs, exponents, weights):
+    rows, width = tokens.shape
+    depth, columns = weights.shape
+    quarter = width // nz
+    total = rows * gathered
+    chunk = total // nz
+    strip = next(s for s in (512, 256, 128) if columns % s == 0)
+    strips = columns // strip
+    vmem = pl.BlockSpec(memory_space=pltpu.VMEM)
+    return pl.pallas_call(
+        functools.partial(kernel, nz, strip),
+        out_shape=jax.ShapeDtypeStruct((chunk, columns), jnp.bfloat16),
+        in_specs=[vmem, vmem, vmem, pl.BlockSpec(memory_space=pl.ANY)],
+        out_specs=vmem,
+        scratch_shapes=[
+            pltpu.VMEM((strips, depth, strip), jnp.bfloat16),
+            pltpu.VMEM((nz, rows, quarter), jnp.bfloat16),
+            pltpu.VMEM((nz, rows, quarter), jnp.bfloat16),
+            pltpu.VMEM((nz, rows, quarter), jnp.bfloat16),
+            pltpu.VMEM((nz, total, quarter), jnp.bfloat16),
+            pltpu.VMEM((strips, nz, chunk, strip), jnp.bfloat16),
+            pltpu.VMEM((strips, nz, chunk, strip), jnp.bfloat16),
+            pltpu.VMEM((strips, nz, chunk, strip), jnp.bfloat16),
+            pltpu.SemaphoreType.DMA((strips,)),
+        ]
+        + [pltpu.SemaphoreType.DMA((PARTS, nz))] * 10
+        + [pltpu.SemaphoreType.DMA((strips, nz))] * 4,
+        compiler_params=pltpu.CompilerParams(
+            collective_id=0, has_side_effects=True, vmem_limit_bytes=60 * 2**20
+        ),
+        cost_estimate=pl.CostEstimate(
+            flops=2 * total * depth * columns, bytes_accessed=2 * depth * columns, transcendentals=0
+        ),
+    )(tokens, signs[None, :], exponents[None, :], weights)
 
 
 def shards(tokens, signs, exponents, weights):
     rows, width = tokens.shape
     members = lax.axis_size("tensor")
+    gathered = lax.axis_size("dp") * lax.axis_size("pipe")
+    if (
+        lax.axis_size("dp") == 2 and lax.axis_size("pipe") == 2 and members > 1
+        and width % (BASE * members) == 0 and rows % (16 * PARTS) == 0
+        and rows * gathered % (16 * members) == 0 and weights.shape[1] % 128 == 0
+        and 2 * width * weights.shape[1] <= 40 * 2**20
+    ):
+        return fused(members, gathered, tokens, signs, exponents, weights)
     signed = tokens * signs.astype(jnp.bfloat16)[None, :]
     mixed = jnp.dot(
         signed, sylvester(width).astype(jnp.bfloat16), preferred_element_type=jnp.float32

time: 239 us -> 89.9 us (0.38)
  matrix products: 106 us -> 0 us
  waiting for transfers between devices: 106 us -> 0 us
  Pallas kernels: 0 us -> 87.8 us
  between operations: 13.5 us -> 0.01 us
  other arithmetic: 6.86 us -> 0 us
  starting transfers between devices: 5.95 us -> 0 us
    dot_general x2 -> x0, matrix products: 106 us -> none  [the longest x1 87.4 us: shards(): jnp.dot(signed, sylvester(width).astype(jnp.bfloat16), preferred_element_...]
    pallas_call x0 -> x1, Pallas kernels: none -> 87.8 us  [fused(): pl.pallas_call(functools.partial(kernel, nz, strip), out_shape=jax.ShapeD...]
    reduce_scatter x1 -> x0, waiting for transfers between devices: 48.2 us -> none  [shards(): lax.psum_scatter(terms.astype(jnp.bfloat16), 'tensor', scatter_dimension=...]
    ppermute x2 -> x0, waiting for transfers between devices: 34.4 us -> none  [partner_2(): return lax.ppermute(value, axis, pairs)]
    all_gather x1 -> x0, waiting for transfers between devices: 23.7 us -> none  [shards(): lax.all_gather(quantized, ('dp', 'pipe'), axis=0, tiled=True)]
    convert_element_type x4 -> x0, other arithmetic: 6.81 us -> none  [the longest x1 4.85 us: shards(): quantized = (soft * scale).astype(jnp.bfloat16)]
    ppermute x2 -> x0, starting transfers between devices: 5.91 us -> none  [partner_2(): return lax.ppermute(value, axis, pairs)]
  transfers between devices with their start and end apart: 4 -> 0, of which waited for: 4 -> 0; matrix products, arithmetic and copies ran while one was open for 0% -> 0% of each run, Pallas kernels for 0% -> 0%
where the time goes in v1:
time: 89.9 us; the launch traced here: 89.7 us
  Pallas kernels  87.8 us (98%)
  local copies, waits for them, and re-layouts  1.92 us (2%)
    pallas_call x1, Pallas kernels, fused(): pl.pallas_call(functools.partial(kernel, nz, strip), out_shape=jax.ShapeD...  87.8 us
    unnamed x1, local copies, waits for them, and re-layouts  1.92 us

profile of v1, /device:TPU:0, one launch (start us, length us, event | category | flops | bytes accessed | tf_op | source)
XLA Modules:
  0.0 89.7 jit_solution(3490902428146340511)
XLA Ops:
  0.0 87.8 %shard_map.46 = bf16[64,4608]{1,0:T(8,128)(2,1)} custom-call(bf16[64,4096]{1,0:T(8,128)(2,1)} %tokens.1, s32[1,4096]{1,0:T(1,128)} %bitcast.2, s32[1,64]{1,0:T(1,128)} %bitcast.3, bf16[4096,4608]{1,0:T(8,128)(2,1)} %weights.1), custom_call_target="tpu_custom_call" | custom-call | flops 9663676416 | bytes 37748736 | tf_op jit(solution)/shard_map/pallas_call | solution.py:283
  87.8 1.9 %copy.6 = bf16[64,4608]{1,0:T(8,128)(2,1)} copy(bf16[64,4608]{1,0:T(8,128)(2,1)} %shard_map.46) | data formatting | bytes 1179648

commit v2 on v1

--- a/solution.py
+++ b/solution.py
@@ -12,6 +12,7 @@
 MESH = pl.DeviceIdType.MESH
 BASE = 256
 PARTS = 2
+CROSS_STEP = 0
 
 
 def partner_2(value, axis, bit):
@@ -70,7 +71,6 @@
     quarter = width // nz
     part_rows = rows // PARTS
     strips = weights.shape[1] // strip
-    chunk = out.shape[0]
     z = lax.axis_index("tensor")
     x = lax.axis_index("dp")
     core = lax.axis_index("pipe")
@@ -99,7 +99,11 @@
             device_id={"tensor": z ^ k}, device_id_type=MESH,
         )
 
-    for h in range(PARTS):
+    def start_mix(h):
+        for k in range(nz - 1, 0, -1):
+            mix_copy(h, k).start()
+
+    def mix(h):
         span = slice(h * part_rows, (h + 1) * part_rows)
         blocks = []
         for a in range(width // BASE):
@@ -108,13 +112,14 @@
         for a, block in enumerate(butterfly(blocks)):
             q, at = divmod(a * BASE, quarter)
             mixed[q, span, at:at + BASE] = (block * jnp.float32(1.0 / math.sqrt(D))).astype(jnp.bfloat16)
-        if h == 0:
-            pl.semaphore_wait(barrier, nz + 1)
-        for k in range(nz - 1, 0, -1):
-            mix_copy(h, k).start()
         taken[z, span] = mixed[z, span]
 
+    mix(0)
+    pl.semaphore_wait(barrier, nz + 1)
+    start_mix(0)
     pl.loop(0, strips)(lambda s: weight_copy(s).start())
+    for h in range(1, PARTS):
+        mix(h)
 
     at_row = lax.broadcasted_iota(jnp.int32, (rows, rows), 0)
     at_col = lax.broadcasted_iota(jnp.int32, (rows, rows), 1)
@@ -124,19 +129,18 @@
     scale = jnp.exp2(power)
     inverse = jnp.exp2(-power)
 
-    mine = (x * 2 + core) * rows
+    def rows_of(owner_x):
+        return pl.ds(pl.multiple_of((owner_x * 2 + core) * part_rows, part_rows), part_rows)
 
     def lev_copy(h, k):
         return pltpu.make_async_remote_copy(
-            src_ref=levels.at[z ^ k, pl.ds(h * part_rows, part_rows)],
-            dst_ref=acts.at[z, pl.ds(pl.multiple_of(mine + h * part_rows, part_rows), part_rows)],
+            src_ref=levels.at[z ^ k, pl.ds(h * part_rows, part_rows)], dst_ref=acts.at[h, z, rows_of(x)],
             send_sem=lev_send.at[h, k], recv_sem=lev_recv.at[h, k],
             device_id={"tensor": z ^ k}, device_id_type=MESH,
         )
 
     def side_copy(h, k, owner_x, target, send, recv):
-        at = (owner_x * 2 + core) * rows + h * part_rows
-        ref = acts.at[z ^ k, pl.ds(pl.multiple_of(at, part_rows), part_rows)]
+        ref = acts.at[h, z ^ k, rows_of(owner_x)]
         return pltpu.make_async_remote_copy(
             src_ref=ref, dst_ref=ref, send_sem=send.at[h, k], recv_sem=recv.at[h, k],
             device_id=target, device_id_type=MESH,
@@ -151,7 +155,7 @@
     def pass_copy(h, k):
         return side_copy(h, k, 1 - x, beside, pass_send, pass_recv)
 
-    for h in range(PARTS):
+    def cross(h):
         span = slice(h * part_rows, (h + 1) * part_rows)
         for k in range(1, nz):
             mix_copy(h, k).wait_recv()
@@ -162,98 +166,127 @@
                 levels[q, span, lanes] = fake_quantize(whole[q], scale[span], inverse[span])
         for k in range(nz - 1, 0, -1):
             lev_copy(h, k).start()
-        acts[z, pl.ds(pl.multiple_of(mine + h * part_rows, part_rows), part_rows)] = levels[z, span]
+        acts[h, z, rows_of(x)] = levels[z, span]
         x_copy(h, 0).start()
         core_copy(h, 0).start()
-
-    steps = [(h, 0) for h in range(PARTS)] + [(h, k) for h in range(PARTS) for k in range(1, nz)]
-    for i in range(len(steps) + 1):
-        if PARTS <= i < len(steps):
-            lev_copy(*steps[i]).wait_recv()
-            x_copy(*steps[i]).start()
-            core_copy(*steps[i]).start()
-        if i > 0:
-            x_copy(*steps[i - 1]).wait_recv()
-            pass_copy(*steps[i - 1]).start()
-    for step in steps:
-        core_copy(*step).wait_recv()
-        pass_copy(*step).wait_recv()
-
-    def right_copy(s, d):
-        return pltpu.make_async_remote_copy(
-            src_ref=terms.at[s, d], dst_ref=from_left.at[s, d],
-            send_sem=right_send.at[s, d], recv_sem=right_recv.at[s, d],
+        if h + 1 < PARTS:
+            start_mix(h + 1)
+
+    def gather(h, k):
+        if k < nz:
+            lev_copy(h, k).wait_recv()
+            x_copy(h, k).start()
+            core_copy(h, k).start()
+        x_copy(h, k - 1).wait_recv()
+        pass_copy(h, k - 1).start()
+        if k == nz:
+            for i in range(nz):
+                core_copy(h, i).wait_recv()
+                pass_copy(h, i).wait_recv()
+
+    cross(0)
+    for k in range(1, nz + 1):
+        gather(0, k)
+
+    def right_copy(u, d):
+        return pltpu.make_async_remote_copy(
+            src_ref=terms.at[u, d], dst_ref=from_left.at[u, d],
+            send_sem=right_send.at[u, d], recv_sem=right_recv.at[u, d],
             device_id={"tensor": lax.rem(z + 1, nz)}, device_id_type=MESH,
         )
 
-    def left_copy(s, d):
-        return pltpu.make_async_remote_copy(
-            src_ref=terms.at[s, d], dst_ref=from_right.at[s, d],
-            send_sem=left_send.at[s, d], recv_sem=left_recv.at[s, d],
+    def left_copy(u, d):
+        return pltpu.make_async_remote_copy(
+            src_ref=terms.at[u, d], dst_ref=from_right.at[u, d],
+            send_sem=left_send.at[u, d], recv_sem=left_recv.at[u, d],
             device_id={"tensor": lax.rem(z + nz - 1, nz)}, device_id_type=MESH,
         )
 
-    def add_in(s, d, arrived):
-        terms[s, d] = (terms[s, d].astype(jnp.float32) + arrived[s, d].astype(jnp.float32)).astype(jnp.bfloat16)
-
-    def when_strip(s, body):
-        pl.when(jnp.logical_and(s >= 0, s < strips))(functools.partial(body, s))
-
-    def multiply(s):
-        weight_copy(s).wait()
-        total = jnp.dot(acts[0], held[s, :quarter], preferred_element_type=jnp.float32)
+    def add_in(u, d, arrived):
+        terms[u, d] = (terms[u, d].astype(jnp.float32) + arrived[u, d].astype(jnp.float32)).astype(jnp.bfloat16)
+
+    units = PARTS * strips
+
+    def when_unit(u, body):
+        pl.when(jnp.logical_and(u >= 0, u < units))(functools.partial(body, u))
+
+    def multiply(u):
+        h, s = lax.div(u, strips), lax.rem(u, strips)
+        pl.when(u < strips)(lambda: weight_copy(u).wait())
+        total = jnp.dot(acts[h, 0], held[s, :quarter], preferred_element_type=jnp.float32)
         for q in range(1, nz):
             total += jnp.dot(
-                acts[q], held[s, q * quarter:(q + 1) * quarter], preferred_element_type=jnp.float32
+                acts[h, q], held[s, q * quarter:(q + 1) * quarter], preferred_element_type=jnp.float32
             )
         for d in range(nz):
-            terms[s, d] = total[d * chunk:(d + 1) * chunk].astype(jnp.bfloat16)
-
-    def hop(at, s):
+            terms[u, d] = total[d * part_rows:(d + 1) * part_rows].astype(jnp.bfloat16)
+
+    def first(u, near):
+        @pl.when(z == 0)
+        def _():
+            for d in (1,) if near else range(nz - 1, 1, -1):
+                right_copy(u, d).start()
+
+        @pl.when(z == nz - 1)
+        def _():
+            for d in (nz - 2,) if near else range(nz - 2):
+                left_copy(u, d).start()
+
+    def hop(at, u):
         @pl.when(z == at)
         def _():
             for d in range(nz - 1, at, -1):
-                if at > 0:
-                    right_copy(s, d).wait_recv()
-                    add_in(s, d, from_left)
-                right_copy(s, d).start()
+                right_copy(u, d).wait_recv()
+                add_in(u, d, from_left)
+                right_copy(u, d).start()
 
         @pl.when(z == nz - 1 - at)
         def _():
             for d in range(nz - 1 - at):
-                if at > 0:
-                    left_copy(s, d).wait_recv()
-                    add_in(s, d, from_right)
-                left_copy(s, d).start()
-
-    def finish(s):
+                left_copy(u, d).wait_recv()
+                add_in(u, d, from_right)
+                left_copy(u, d).start()
+
+    def finish(u):
+        h, s = lax.div(u, strips), lax.rem(u, strips)
+        at = pl.ds(pl.multiple_of(h * part_rows, part_rows), part_rows)
         cols = pl.ds(pl.multiple_of(s * strip, strip), strip)
-        own = terms[s, z].astype(jnp.float32)
+        own = terms[u, z].astype(jnp.float32)
 
         @pl.when(z == 0)
         def _():
-            left_copy(s, z).wait_recv()
-            out[:, cols] = (own + from_right[s, z].astype(jnp.float32)).astype(out.dtype)
+            left_copy(u, z).wait_recv()
+            out[at, cols] = (own + from_right[u, z].astype(jnp.float32)).astype(out.dtype)
 
         @pl.when(z == nz - 1)
         def _():
-            right_copy(s, z).wait_recv()
-            out[:, cols] = (own + from_left[s, z].astype(jnp.float32)).astype(out.dtype)
+            right_copy(u, z).wait_recv()
+            out[at, cols] = (own + from_left[u, z].astype(jnp.float32)).astype(out.dtype)
 
         @pl.when(jnp.logical_and(z > 0, z < nz - 1))
         def _():
-            right_copy(s, z).wait_recv()
-            left_copy(s, z).wait_recv()
-            out[:, cols] = (
-                own + from_left[s, z].astype(jnp.float32) + from_right[s, z].astype(jnp.float32)
+            right_copy(u, z).wait_recv()
+            left_copy(u, z).wait_recv()
+            out[at, cols] = (
+                own + from_left[u, z].astype(jnp.float32) + from_right[u, z].astype(jnp.float32)
             ).astype(out.dtype)
 
-    @pl.loop(0, strips + nz - 1)
+    near_lag = strips
+    last_lag = max(near_lag + 1, 2 * (nz - 1))
+
+    @pl.loop(0, units + last_lag)
     def _(t):
-        when_strip(t, multiply)
-        for at in range(nz - 1):
-            when_strip(t - at, functools.partial(hop, at))
-        when_strip(t - (nz - 1), finish)
+        for h in range(1, PARTS):
+            before = (h - 1) * strips
+            pl.when(t == before + CROSS_STEP)(functools.partial(cross, h))
+            for k in range(1, nz + 1):
+                pl.when(t == before + min(CROSS_STEP + k, strips))(functools.partial(gather, h, k))
+        when_unit(t, multiply)
+        when_unit(t, lambda u: first(u, False))
+        when_unit(t - near_lag, lambda u: first(u, True))
+        for at in range(1, nz - 1):
+            when_unit(t - 2 * at, functools.partial(hop, at))
+        when_unit(t - last_lag, finish)
 
     for h in range(PARTS):
         for k in range(nz):
@@ -264,11 +297,11 @@
             core_copy(h, k).wait_send()
             pass_copy(h, k).wait_send()
 
-    @pl.loop(0, strips)
-    def _(s):
+    @pl.loop(0, units)
+    def _(u):
         for d in range(nz):
-            pl.when(z < d)(lambda d=d: right_copy(s, d).wait_send())
-            pl.when(z > d)(lambda d=d: left_copy(s, d).wait_send())
+            pl.when(z < d)(lambda d=d: right_copy(u, d).wait_send())
+            pl.when(z > d)(lambda d=d: left_copy(u, d).wait_send())
 
 
 def fused(nz, gathered, tokens, signs, exponents, weights):
@@ -276,13 +309,13 @@
     depth, columns = weights.shape
     quarter = width // nz
     total = rows * gathered
-    chunk = total // nz
-    strip = next(s for s in (512, 256, 128) if columns % s == 0)
+    strip = next(s for s in (1536, 768, 512, 256, 128) if columns % s == 0)
     strips = columns // strip
+    units = PARTS * strips
     vmem = pl.BlockSpec(memory_space=pltpu.VMEM)
     return pl.pallas_call(
         functools.partial(kernel, nz, strip),
-        out_shape=jax.ShapeDtypeStruct((chunk, columns), jnp.bfloat16),
+        out_shape=jax.ShapeDtypeStruct((rows, columns), jnp.bfloat16),
         in_specs=[vmem, vmem, vmem, pl.BlockSpec(memory_space=pl.ANY)],
         out_specs=vmem,
         scratch_shapes=[
@@ -290,14 +323,14 @@
             pltpu.VMEM((nz, rows, quarter), jnp.bfloat16),
             pltpu.VMEM((nz, rows, quarter), jnp.bfloat16),
             pltpu.VMEM((nz, rows, quarter), jnp.bfloat16),
-            pltpu.VMEM((nz, total, quarter), jnp.bfloat16),
-            pltpu.VMEM((strips, nz, chunk, strip), jnp.bfloat16),
-            pltpu.VMEM((strips, nz, chunk, strip), jnp.bfloat16),
-            pltpu.VMEM((strips, nz, chunk, strip), jnp.bfloat16),
+            pltpu.VMEM((PARTS, nz, total // PARTS, quarter), jnp.bfloat16),
+        ]
+        + [pltpu.VMEM((units, nz, rows // PARTS, strip), jnp.bfloat16)] * 3
+        + [
             pltpu.SemaphoreType.DMA((strips,)),
         ]
         + [pltpu.SemaphoreType.DMA((PARTS, nz))] * 10
-        + [pltpu.SemaphoreType.DMA((strips, nz))] * 4,
+        + [pltpu.SemaphoreType.DMA((units, nz))] * 4,
         compiler_params=pltpu.CompilerParams(
             collective_id=0, has_side_effects=True, vmem_limit_bytes=60 * 2**20
         ),
@@ -312,9 +345,9 @@
     members = lax.axis_size("tensor")
     gathered = lax.axis_size("dp") * lax.axis_size("pipe")
     if (
-        lax.axis_size("dp") == 2 and lax.axis_size("pipe") == 2 and members > 1
+        lax.axis_size("dp") == 2 and lax.axis_size("pipe") == 2 and members == gathered
         and width % (BASE * members) == 0 and rows % (16 * PARTS) == 0
-        and rows * gathered % (16 * members) == 0 and weights.shape[1] % 128 == 0
+        and weights.shape[1] % 128 == 0
         and 2 * width * weights.shape[1] <= 40 * 2**20
     ):
         return fused(members, gathered, tokens, signs, exponents, weights)

time: 89.9 us -> 76.8 us (0.85)
  Pallas kernels: 87.8 us -> 74.7 us
    pallas_call x1, Pallas kernels: 87.8 us -> 74.7 us  [fused(): pl.pallas_call(functools.partial(kernel, nz, strip), out_shape=jax.ShapeD...]
where the time goes in v2:
time: 76.8 us; the launch traced here: 76.7 us
  Pallas kernels  74.7 us (97%)
  local copies, waits for them, and re-layouts  1.92 us (2%)
    pallas_call x1, Pallas kernels, fused(): pl.pallas_call(functools.partial(kernel, nz, strip), out_shape=jax.ShapeD...  74.7 us
    unnamed x1, local copies, waits for them, and re-layouts  1.92 us

profile of v2, /device:TPU:0, one launch (start us, length us, event | category | flops | bytes accessed | tf_op | source)
XLA Modules:
  0.0 76.7 jit_solution(2478501872715174087)
XLA Ops:
  0.0 74.7 %shard_map.46 = bf16[64,4608]{1,0:T(8,128)(2,1)} custom-call(bf16[64,4096]{1,0:T(8,128)(2,1)} %tokens.1, s32[1,4096]{1,0:T(1,128)} %bitcast.2, s32[1,64]{1,0:T(1,128)} %bitcast.3, bf16[4096,4608]{1,0:T(8,128)(2,1)} %weights.1), custom_call_target="tpu_custom_call" | custom-call | flops 9663676416 | bytes 37748736 | tf_op jit(solution)/shard_map/pallas_call | solution.py:316
  74.7 1.9 %copy.6 = bf16[64,4608]{1,0:T(8,128)(2,1)} copy(bf16[64,4608]{1,0:T(8,128)(2,1)} %shard_map.46) | data formatting | bytes 1179648

commit v3 on v2

--- a/solution.py
+++ b/solution.py
@@ -272,7 +272,7 @@
             ).astype(out.dtype)
 
     near_lag = strips
-    last_lag = max(near_lag + 1, 2 * (nz - 1))
+    last_lag = max(near_lag + 1, nz)
 
     @pl.loop(0, units + last_lag)
     def _(t):
@@ -285,7 +285,7 @@
         when_unit(t, lambda u: first(u, False))
         when_unit(t - near_lag, lambda u: first(u, True))
         for at in range(1, nz - 1):
-            when_unit(t - 2 * at, functools.partial(hop, at))
+            when_unit(t - at, functools.partial(hop, at))
         when_unit(t - last_lag, finish)
 
     for h in range(PARTS):

time: 76.8 us -> 75.6 us (0.984)
  Pallas kernels: 74.7 us -> 73.5 us
    pallas_call x1, Pallas kernels: 74.7 us -> 73.5 us  [fused(): pl.pallas_call(functools.partial(kernel, nz, strip), out_shape=jax.ShapeD...]
where the time goes in v3:
time: 75.6 us; the launch traced here: 75.5 us
  Pallas kernels  73.5 us (97%)
  local copies, waits for them, and re-layouts  1.92 us (3%)
    pallas_call x1, Pallas kernels, fused(): pl.pallas_call(functools.partial(kernel, nz, strip), out_shape=jax.ShapeD...  73.5 us
    unnamed x1, local copies, waits for them, and re-layouts  1.92 us

profile of v3, /device:TPU:0, one launch (start us, length us, event | category | flops | bytes accessed | tf_op | source)
XLA Modules:
  0.0 75.5 jit_solution(17003778778410181524)
XLA Ops:
  0.0 73.5 %shard_map.46 = bf16[64,4608]{1,0:T(8,128)(2,1)} custom-call(bf16[64,4096]{1,0:T(8,128)(2,1)} %tokens.1, s32[1,4096]{1,0:T(1,128)} %bitcast.2, s32[1,64]{1,0:T(1,128)} %bitcast.3, bf16[4096,4608]{1,0:T(8,128)(2,1)} %weights.1), custom_call_target="tpu_custom_call" | custom-call | flops 9663676416 | bytes 37748736 | tf_op jit(solution)/shard_map/pallas_call | solution.py:316
  73.5 1.9 %copy.6 = bf16[64,4608]{1,0:T(8,128)(2,1)} copy(bf16[64,4608]{1,0:T(8,128)(2,1)} %shard_map.46) | data formatting | bytes 1179648
